TPU v7x, 512 devices: a whole 4x4x16 slice. The times are simulated.
512 devices in a mesh: row: 32 (over z, x_lo), col: 16 (over y, x_hi, core).
Axes of the slice: x: 4 (x_hi: 2, x_lo: 2; x = x_hi * 2 + x_lo), y: 4, z: 16, core: 2. Of those that a mesh axis runs over, the one named last changes fastest.
Arguments:
- x_window: bfloat16 [3, 2048, 512], P(None, 'row', 'col'), may hold values from -6 to 6
- y_window: float32 [3, 2048], P(None, 'row'), may hold values from -6 to 6
- block_order: int32 [3], replicated, may hold values from 0 to 2, each once
- diag_inverse: bfloat16 [3, 2048, 2048], P(None, 'row'), may hold values from -0.5 to 1.5, as said below
- panel_window: bfloat16 [3, 2048, 2048], P(None, 'row', 'col'), may hold values from -0.078125 to 0.078125
- panel_trail: bfloat16 [4096, 3, 2048], P('row', None, 'col'), may hold values from -0.078125 to 0.078125
- x_trail: bfloat16 [4096, 512], P('row', 'col'), may hold values from -6 to 6
- y_trail: float32 [4096], P('row'), may hold values from -6 to 6
Outputs:
- whitened: bfloat16 [3, 2048, 512], P(None, 'row', 'col')
- white_resp: bfloat16 [3, 2048], P(None, 'row')
- trail_rhs: float32 [4096, 512], P('row', 'col')
- trail_resp: float32 [4096], P('row')
- normal_part: float32 [512, 512], P('row')
- right_part: float32 [512], P('row')
Inputs may be any that keep to these rules, and one draw needn't show every extreme that they name: Each diag_inverse[s] is lower triangular with a positive diagonal.
All inputs are finite; a program needn't handle non-finite values.
Results may differ from a plain program's by a relative error of at most 0.014.
Values may be sent and summed in bfloat16 or wider, within the bound.
A program may use at most 64 MiB of HBM per device.

v0:
```python
import jax
import jax.numpy as jnp
from jax import lax
from jax.sharding import PartitionSpec as P


def shards(
    x_window, y_window, block_order, diag_inverse, panel_window, panel_trail, x_trail, y_trail
):
    steps = x_window.shape[0]
    own_rows = x_window.shape[1]
    own_cols = x_window.shape[2]
    width = panel_window.shape[2]
    block_rows = own_rows * lax.axis_size("row")
    full_cols = own_cols * lax.axis_size("col")
    normal_rows = full_cols // lax.axis_size("row")
    col_start = lax.axis_index("col") * width
    normal_start = lax.axis_index("row") * normal_rows
    trail_rows = x_trail.shape[0]
    solved_cols = []
    solved_resp = []
    out_tiles = []
    out_resp = []
    trail_total = jnp.zeros((trail_rows, full_cols), jnp.float32)
    trail_resp_total = jnp.zeros((trail_rows,), jnp.float32)
    gram = jnp.zeros((normal_rows, full_cols), jnp.float32)
    right = jnp.zeros((normal_rows,), jnp.float32)
    for s in range(steps):
        stored = block_order[s]
        pending = lax.dynamic_index_in_dim(x_window, stored, 0, keepdims=False).astype(jnp.float32)
        pending_resp = lax.dynamic_index_in_dim(y_window, stored, 0, keepdims=False)
        if s > 0:
            first = s * (s - 1) // 2
            factors = panel_window[first : first + s]
            earlier = jnp.stack(solved_cols)
            earlier_resp = jnp.stack(solved_resp)
            update = jnp.einsum("trw,twp->rp", factors, earlier, preferred_element_type=jnp.float32)
            update_resp = jnp.einsum(
                "trw,tw->r", factors, earlier_resp, preferred_element_type=jnp.float32
            )
            pending = pending - lax.psum_scatter(update, "col", scatter_dimension=1, tiled=True)
            pending_resp = pending_resp - lax.psum(update_resp, "col")
        residual = pending.astype(jnp.bfloat16)
        resid_resp = pending_resp.astype(jnp.bfloat16)
        whole, whole_resp = (
            lax.all_gather(residual, "row", axis=0, tiled=True),
            lax.all_gather(resid_resp, "row", axis=0, tiled=True),
        )
        inverse = diag_inverse[s]
        tile = jnp.dot(inverse, whole, preferred_element_type=jnp.float32).astype(jnp.bfloat16)
        tile_resp = jnp.dot(inverse, whole_resp, preferred_element_type=jnp.float32).astype(
            jnp.bfloat16
        )
        out_tiles.append(tile)
        out_resp.append(tile_resp)
        all_rows, all_resp = (
            lax.all_gather(tile, "row", axis=0, tiled=True),
            lax.all_gather(tile_resp, "row", axis=0, tiled=True),
        )
        mine = lax.all_to_all(all_rows, "col", split_axis=0, concat_axis=1, tiled=True)
        mine_resp = lax.dynamic_slice_in_dim(all_resp, col_start, width, 0)
        solved_cols.append(mine)
        solved_resp.append(mine_resp)
        factor_rows = panel_trail[:, s, :]
        trail_total = trail_total + jnp.dot(factor_rows, mine, preferred_element_type=jnp.float32)
        trail_resp_total = trail_resp_total + jnp.dot(
            factor_rows, mine_resp, preferred_element_type=jnp.float32
        )
        slab = lax.dynamic_slice_in_dim(mine, normal_start, normal_rows, 1)
        gram = gram + lax.dot_general(
            slab, mine, (((0,), (0,)), ((), ())), preferred_element_type=jnp.float32
        )
        right = right + lax.dot_general(
            slab, mine_resp, (((0,), (0,)), ((), ())), preferred_element_type=jnp.float32
        )
    summed = lax.psum(trail_total.astype(jnp.bfloat16), "col").astype(jnp.float32)
    share = lax.dynamic_slice_in_dim(summed, lax.axis_index("col") * own_cols, own_cols, 1)
    trail_rhs = x_trail.astype(jnp.float32) - share
    gram, right, resp_sum = lax.psum((gram, right, trail_resp_total), "col")
    trail_resp = y_trail - resp_sum
    scale = 1.0 / (steps * block_rows)
    whitened = jnp.stack(out_tiles)
    white_resp = jnp.stack(out_resp)
    return (whitened, white_resp, trail_rhs, trail_resp, gram * scale, right * scale)


def solution(mesh):
    in_specs = (
        P(None, "row", "col"),
        P(None, "row"),
        P(),
        P(None, "row", None),
        P(None, "row", "col"),
        P("row", None, "col"),
        P("row", "col"),
        P("row"),
    )
    out_specs = (
        P(None, "row", "col"),
        P(None, "row"),
        P("row", "col"),
        P("row"),
        P("row", None),
        P("row"),
    )
    return jax.shard_map(shards, mesh=mesh, in_specs=in_specs, out_specs=out_specs, check_vma=False)
```

profile of v0, /device:TPU:1, one launch (start us, length us, event | category | flops | bytes accessed | tf_op | source)
XLA Modules:
  0.0 1263.4 jit_solution(17524989272356092082)
XLA Ops:
  7.2 1.4 fusion.84
  14.5 61.7 %all-gather = bf16[1,2048,32]{2,0,1:T(2,128)(2,1)S(1)} all-gather(bf16[1,64,32]{2,0,1:T(2,128)(2,1)S(1)} %copy.62), channel_id=2, replica_groups=mesh['row'=32,'col'=16] {'row'}, dimensions={1}, use_global_device_ids=true | all-gather | bytes 135168 | tf_op jit(solution)/shard_map/all_gather | solution.py:46
  76.2 0.5 copy.42
  76.8 0.6 copy-done
  77.4 0.2 fusion.2
  77.5 46.4 %all-gather.2 = bf16[32,64,32]{1,2,0:T(8,128)(2,1)S(1)} all-gather(bf16[1,64,32]{1,2,0:T(8,128)(2,1)S(1)} %fusion.2), channel_id=1, replica_groups=mesh['row'=32,'col'=16] {'row'}, dimensions={0}, use_global_device_ids=true | all-gather | bytes 135168 | tf_op jit(solution)/shard_map/all_gather | solution.py:57
  124.2 0.7 copy.45
  124.9 34.9 %all-to-all-start = ((bf16[16,128,32]{1,2,0:T(8,128)(2,1)}), bf16[16,128,32]{1,2,0:T(8,128)(2,1)S(1)}, u32[]{:S(2)}, u32[]{:S(2)}) async-start(bf16[16,128,32]{1,2,0:T(8,128)(2,1)} %copy.45), calls=%async_computation | async-start | bytes 262144 | tf_op jit(solution)/shard_map/all_to_all | solution.py:60
  159.9 0.6 copy-done.5
  160.5 1.3 dynamic-slice
  162.4 0.2 dynamic-update-slice
  162.7 47.3 %all-reduce = bf16[2048]{0:T(1024)(128)(2,1)S(1)} all-reduce(bf16[2048]{0:T(1024)(128)(2,1)S(1)} %dynamic-update-slice), channel_id=3, replica_groups=mesh['row'=32,'col'=16] {'row'}, use_global_device_ids=true, to_apply=%add | all-reduce | flops 2048 | bytes 8192 | tf_op jit(solution)/shard_map/all_gather | solution.py:47
  210.2 0.2 dynamic-update-slice.1
  210.4 46.7 %all-reduce.1 = bf16[2048]{0:T(1024)(128)(2,1)S(1)} all-reduce(bf16[2048]{0:T(1024)(128)(2,1)S(1)} %dynamic-update-slice.1), channel_id=1, replica_groups=mesh['row'=32,'col'=16] {'row'}, use_global_device_ids=true, to_apply=%add.1 | all-reduce | flops 2048 | bytes 8192
  257.2 0.2 convolution_bitcast_fusion.9
  257.4 60.9 %psum.42 = f32[64]{0:T(128)S(1)} all-reduce(f32[64]{0:T(128)S(1)} %convolution_bitcast_fusion.9), channel_id=1, replica_groups=mesh['row'=32,'col'=16] {'col'}, use_global_device_ids=true, to_apply=%region_2.3 | all-reduce | flops 64 | bytes 512 | tf_op jit(solution)/shard_map/psum | solution.py:42
  318.3 0.2 dynamic-update-slice.2
  318.5 47.1 %all-reduce.2 = bf16[2048]{0:T(1024)(128)(2,1)S(1)} all-reduce(bf16[2048]{0:T(1024)(128)(2,1)S(1)} %dynamic-update-slice.2), channel_id=1, replica_groups=mesh['row'=32,'col'=16] {'row'}, use_global_device_ids=true, to_apply=%add.2 | all-reduce | flops 2048 | bytes 8192
  365.8 0.2 dynamic-update-slice.3
  366.0 47.2 %all-reduce.3 = bf16[2048]{0:T(1024)(128)(2,1)S(1)} all-reduce(bf16[2048]{0:T(1024)(128)(2,1)S(1)} %dynamic-update-slice.3), channel_id=1, replica_groups=mesh['row'=32,'col'=16] {'row'}, use_global_device_ids=true, to_apply=%add.3 | all-reduce | flops 2048 | bytes 8192
  413.4 60.5 %psum.43 = f32[64]{0:T(128)S(1)} all-reduce(f32[64]{0:T(128)S(1)} %convolution_bitcast_fusion.2), channel_id=1, replica_groups=mesh['row'=32,'col'=16] {'col'}, use_global_device_ids=true, to_apply=%region_3.4 | all-reduce | flops 64 | bytes 512 | tf_op jit(solution)/shard_map/psum | solution.py:42
  473.9 0.2 dynamic-update-slice.4
  474.2 47.3 %all-reduce.4 = bf16[2048]{0:T(1024)(128)(2,1)S(1)} all-reduce(bf16[2048]{0:T(1024)(128)(2,1)S(1)} %dynamic-update-slice.4), channel_id=1, replica_groups=mesh['row'=32,'col'=16] {'row'}, use_global_device_ids=true, to_apply=%add.4 | all-reduce | flops 2048 | bytes 8192
  521.6 0.2 fusion.9
  521.7 0.2 dynamic-update-slice.5
  521.9 46.9 %all-reduce.5 = bf16[2048]{0:T(1024)(128)(2,1)S(1)} all-reduce(bf16[2048]{0:T(1024)(128)(2,1)S(1)} %dynamic-update-slice.5), channel_id=1, replica_groups=mesh['row'=32,'col'=16] {'row'}, use_global_device_ids=true, to_apply=%add.5 | all-reduce | flops 2048 | bytes 8192
  568.9 0.2 convolution_bitcast_fusion.8
  569.0 0.2 fusion.8
  569.2 0.2 fusion.7
  569.6 0.6 pad_maximum_fusion.1
  570.4 0.2 convolution_bitcast_fusion.5
  570.6 0.8 copy.58
  571.6 0.2 fusion.35
  571.7 105.4 %reduce-scatter.7.cloned.1.call-done = f32[32,64]{1,0:T(8,128)} async-done(((f32[512,64]{1,0:T(8,128)}), f32[32,64]{1,0:T(8,128)}) %reduce-scatter.7.cloned.1.call-update) | async-done | bytes 8208
  677.1 0.8 copy.59
  678.0 50.2 %all-gather.3 = bf16[32,64,32]{1,2,0:T(8,128)(2,1)S(1)} all-gather(bf16[1,64,32]{1,2,0:T(8,128)(2,1)S(1)} %copy.46), channel_id=1, replica_groups=mesh['row'=32,'col'=16] {'row'}, dimensions={0}, use_global_device_ids=true | all-gather | bytes 135168 | tf_op jit(solution)/shard_map/all_gather | solution.py:46
  728.3 0.3 reshape.65
  728.6 0.2 fusion.3
  728.7 46.4 %all-gather.4 = bf16[32,64,32]{1,2,0:T(8,128)(2,1)S(1)} all-gather(bf16[1,64,32]{1,2,0:T(8,128)(2,1)S(1)} %fusion.3), channel_id=1, replica_groups=mesh['row'=32,'col'=16] {'row'}, dimensions={0}, use_global_device_ids=true | all-gather | bytes 135168 | tf_op jit(solution)/shard_map/all_gather | solution.py:57
  775.4 0.7 copy.50
  776.1 34.8 %all-to-all-start.1 = ((bf16[16,128,32]{1,2,0:T(8,128)(2,1)}), bf16[16,128,32]{1,2,0:T(8,128)(2,1)S(1)}, u32[]{:S(2)}, u32[]{:S(2)}) async-start(bf16[16,128,32]{1,2,0:T(8,128)(2,1)} %copy.50), calls=%async_computation.1 | async-start | bytes 262144 | tf_op jit(solution)/shard_map/all_to_all | solution.py:60
  811.0 7.5 all-to-all-done.1
  818.8 0.8 copy.60
  819.6 0.2 convolution_add_fusion.1
  820.0 81.2 %reduce-scatter.9.cloned.1.call-done = f32[32,64]{1,0:T(8,128)} async-done(((f32[512,64]{1,0:T(8,128)}), f32[32,64]{1,0:T(8,128)}) %reduce-scatter.9.cloned.1.call-update) | async-done | bytes 8208
  901.2 0.8 copy.61
  902.1 50.2 %all-gather.5 = bf16[32,64,32]{1,2,0:T(8,128)(2,1)S(1)} all-gather(bf16[1,64,32]{1,2,0:T(8,128)(2,1)S(1)} %copy.53), channel_id=1, replica_groups=mesh['row'=32,'col'=16] {'row'}, dimensions={0}, use_global_device_ids=true | all-gather | bytes 135168 | tf_op jit(solution)/shard_map/all_gather | solution.py:46
  952.3 0.3 reshape.69
  952.6 0.2 fusion.4
  952.8 46.4 %all-gather.6 = bf16[32,64,32]{1,2,0:T(8,128)(2,1)S(1)} all-gather(bf16[1,64,32]{1,2,0:T(8,128)(2,1)S(1)} %fusion.4), channel_id=1, replica_groups=mesh['row'=32,'col'=16] {'row'}, dimensions={0}, use_global_device_ids=true | all-gather | bytes 135168 | tf_op jit(solution)/shard_map/all_gather | solution.py:57
  999.5 0.7 copy.56
  1000.1 34.8 %all-to-all-start.2 = ((bf16[16,128,32]{1,2,0:T(8,128)(2,1)}), bf16[16,128,32]{1,2,0:T(8,128)(2,1)S(1)}, u32[]{:S(2)}, u32[]{:S(2)}) async-start(bf16[16,128,32]{1,2,0:T(8,128)(2,1)} %copy.56), calls=%async_computation.2 | async-start | bytes 262144 | tf_op jit(solution)/shard_map/all_to_all | solution.py:60
  1035.0 0.2 fusion.6
  1035.1 0.6 pad_maximum_fusion
  1035.8 6.8 all-to-all-done.2
  1042.6 0.2 fusion.5
  1042.9 60.2 %all-reduce.6 = (f32[128]{0:T(128)S(1)}, f32[16,512]{1,0:T(8,128)S(1)}, f32[16]{0:T(128)S(1)}) all-reduce(f32[128]{0:T(128)S(1)} %fusion.7, f32[16,512]{1,0:T(8,128)S(1)} %convolution_add_fusion.2, f32[16]{0:T(128)S(1)} %fusion.5), channel_id=1, replica_groups=mesh['row'=32,'col'=16] {'col'}, use_global_device_ids=true, to_apply=%region_5.6 | all-reduce | flops 8336 | bytes 66688 | tf_op jit(solution)/shard_map/psum | solution.py:79
  1103.1 0.6 broadcast_multiply_fusion
  1103.7 0.8 fusion.1
  1104.6 0.6 copy-done.6
  1105.3 0.5 sub.23
  1105.8 0.5 broadcast_multiply_fusion.1
  1106.3 149.3 %all-reduce.9.cloned.1.call-done = bf16[128,512]{0,1:T(8,128)(2,1)} async-done(((bf16[128,512]{0,1:T(8,128)(2,1)}), bf16[128,512]{0,1:T(8,128)(2,1)}) %all-reduce.9.cloned.1.call-update) | async-done | bytes 131088 | tf_op jit(solution)/shard_map/psum | solution.py:76
  1255.6 1.3 convert_subtract_fusion.2
  (59 shorter events, 3.3 us)
Async XLA Ops:
  7.2 7.2 copy-start.3
  76.2 1.1 copy-start
  124.9 445.3 %all-to-all-start = ((bf16[16,128,32]{1,2,0:T(8,128)(2,1)}), bf16[16,128,32]{1,2,0:T(8,128)(2,1)S(1)}, u32[]{:S(2)}, u32[]{:S(2)}) async-start(bf16[16,128,32]{1,2,0:T(8,128)(2,1)} %copy.45), calls=%async_computation | async-start | bytes 262144 | tf_op jit(solution)/shard_map/all_to_all | solution.py:60
  159.8 0.7 copy-start.5
  159.8 517.3 %reduce-scatter.7.cloned.1.call-start = ((), (), s32[]{:S(2)}) async-start(), calls=%async_computation.6 | async-start | bytes 278528
  210.0 47.2 %copy-start.2 = (bf16[3,64,128]{2,1,0:T(8,128)(2,1)S(1)}, bf16[3,64,128]{2,1,0:T(8,128)(2,1)}, u32[]{:S(2)}) copy-start(bf16[3,64,128]{2,1,0:T(8,128)(2,1)} %param.12) | copy-start | bytes 147460
  521.6 47.3 %copy-start.1 = (bf16[128,3,128]{2,0,1:T(8,128)(2,1)S(1)}, bf16[128,3,128]{2,0,1:T(8,128)(2,1)}, u32[]{:S(2)}) copy-start(bf16[128,3,128]{2,0,1:T(8,128)(2,1)} %param.13) | copy-start | bytes 294916
  776.1 42.4 %all-to-all-start.1 = ((bf16[16,128,32]{1,2,0:T(8,128)(2,1)}), bf16[16,128,32]{1,2,0:T(8,128)(2,1)S(1)}, u32[]{:S(2)}, u32[]{:S(2)}) async-start(bf16[16,128,32]{1,2,0:T(8,128)(2,1)} %copy.50), calls=%async_computation.1 | async-start | bytes 262144 | tf_op jit(solution)/shard_map/all_to_all | solution.py:60
  810.8 90.3 %reduce-scatter.9.cloned.1.call-start = ((), (), s32[]{:S(2)}) async-start(), calls=%async_computation.7 | async-start | bytes 278528
  1000.1 42.4 %all-to-all-start.2 = ((bf16[16,128,32]{1,2,0:T(8,128)(2,1)}), bf16[16,128,32]{1,2,0:T(8,128)(2,1)S(1)}, u32[]{:S(2)}, u32[]{:S(2)}) async-start(bf16[16,128,32]{1,2,0:T(8,128)(2,1)} %copy.56), calls=%async_computation.2 | async-start | bytes 262144 | tf_op jit(solution)/shard_map/all_to_all | solution.py:60
  1034.9 220.7 %all-reduce.9.cloned.1.call-start = ((), (), s32[]{:S(2)}) async-start(), calls=%async_computation.5 | async-start | bytes 262144 | tf_op jit(solution)/shard_map/psum | solution.py:76
  1104.6 151.0 %copy-start.4 = (bf16[128,32]{0,1:T(8,128)(2,1)S(1)}, bf16[128,32]{0,1:T(8,128)(2,1)}, u32[]{:S(2)}) copy-start(bf16[128,32]{0,1:T(8,128)(2,1)} %param.14) | copy-start | bytes 24580
  1104.6 0.7 copy-start.6
Sparse Core Ops, SparseCore 0:
  571.6 105.5 reduce-scatter.6
  819.8 81.3 reduce-scatter.8
  1104.7 150.7 all-reduce.8
where the time goes:
time: 1260 us
  blocking collectives  765 us (61%)
  waiting for transfers between devices  350 us (28%)
  starting transfers between devices  105 us (8%)
  between operations  20.4 us (2%)
  local copies, waits for them, and re-layouts  14.1 us (1%)
    unnamed x5, blocking collectives  235 us
    unnamed x5, waiting for transfers between devices  187 us
    all_gather x3, blocking collectives, shards(): lax.all_gather(residual, 'row', axis=0, tiled=True)  162 us
    psum x1, waiting for transfers between devices, shards(): lax.psum(trail_total.astype(jnp.bfloat16), 'col').astype(jnp.float32)  149 us
    all_gather x3, blocking collectives, shards(): lax.all_gather(tile, 'row', axis=0, tiled=True)  139 us
    psum x2, blocking collectives, shards(): pending_resp = pending_resp - lax.psum(update_resp, 'col')  121 us
    all_to_all x3, starting transfers between devices, shards(): lax.all_to_all(all_rows, 'col', split_axis=0, concat_axis=1, tiled=True)  104 us
    psum x1, blocking collectives, shards(): gram, right, resp_sum = lax.psum((gram, right, trail_resp_total), 'col')  60.2 us
  transfers between devices with their start and end apart: 6, of which 5 were waited for; matrix products, arithmetic and copies ran while one was open for 1% of the time, Pallas kernels for 0%

commit v1 on v0

--- a/solution.py
+++ b/solution.py
@@ -54,7 +54,9 @@
         out_tiles.append(tile)
         out_resp.append(tile_resp)
         all_rows, all_resp = (
-            lax.all_gather(tile, "row", axis=0, tiled=True),
+            jnp.concatenate(
+                lax.all_to_all(jnp.stack([tile] * lax.axis_size("row")), "row", 0, 0), axis=0
+            ),
             lax.all_gather(tile_resp, "row", axis=0, tiled=True),
         )
         mine = lax.all_to_all(all_rows, "col", split_axis=0, concat_axis=1, tiled=True)

time: 1260 us -> 1070 us (0.85)
  blocking collectives: 765 us -> 620 us
  waiting for transfers between devices: 350 us -> 288 us
    all_gather x3 -> x0, blocking collectives: 139 us -> none  [shards(): lax.all_gather(tile, 'row', axis=0, tiled=True)]
    unnamed x5, waiting for transfers between devices: 187 us -> 119 us
    all_to_all x0 -> x3, starting transfers between devices: none -> 26.5 us  [shards(): lax.all_to_all(jnp.stack([tile] * lax.axis_size('row')), 'row', 0, 0)]
    all_to_all x3, starting transfers between devices: 104 us -> 88.2 us  [shards(): lax.all_to_all(all_rows, 'col', split_axis=0, concat_axis=1, tiled=True)]
    psum x2, blocking collectives: 121 us -> 107 us  [shards(): pending_resp = pending_resp - lax.psum(update_resp, 'col')]
    all_to_all x0 -> x3, waiting for transfers between devices: none -> 13.1 us  [shards(): lax.all_to_all(jnp.stack([tile] * lax.axis_size('row')), 'row', 0, 0)]
  transfers between devices with their start and end apart: 6 -> 9, of which waited for: 5 -> 6; matrix products, arithmetic and copies ran while one was open for 1% -> 1% of each run, Pallas kernels for 0% -> 0%
where the time goes in v1:
time: 1070 us
  blocking collectives  620 us (58%)
  waiting for transfers between devices  288 us (27%)
  starting transfers between devices  115 us (11%)
  between operations  20.5 us (2%)
  local copies, waits for them, and re-layouts  17.5 us (2%)
    unnamed x5, blocking collectives  239 us
    all_gather x3, blocking collectives, shards(): lax.all_gather(residual, 'row', axis=0, tiled=True)  162 us
    psum x1, waiting for transfers between devices, shards(): lax.psum(trail_total.astype(jnp.bfloat16), 'col').astype(jnp.float32)  142 us
    unnamed x5, waiting for transfers between devices  119 us
    psum x2, blocking collectives, shards(): pending_resp = pending_resp - lax.psum(update_resp, 'col')  107 us
    all_to_all x3, starting transfers between devices, shards(): lax.all_to_all(all_rows, 'col', split_axis=0, concat_axis=1, tiled=True)  88.2 us
    psum x1, blocking collectives, shards(): gram, right, resp_sum = lax.psum((gram, right, trail_resp_total), 'col')  60.2 us
    all_gather x1, blocking collectives, shards(): lax.all_gather(resid_resp, 'row', axis=0, tiled=True)  50.5 us
  transfers between devices with their start and end apart: 9, of which 6 were waited for; matrix products, arithmetic and copies ran while one was open for 1% of the time, Pallas kernels for 0%

profile of v1, /device:TPU:1, one launch (start us, length us, event | category | flops | bytes accessed | tf_op | source)
XLA Modules:
  0.0 1069.5 jit_solution(14413445179035576693)
XLA Ops:
  7.2 1.4 fusion.81
  14.5 61.7 %all-gather = bf16[1,2048,32]{2,0,1:T(2,128)(2,1)S(1)} all-gather(bf16[1,64,32]{2,0,1:T(2,128)(2,1)S(1)} %copy.71), channel_id=2, replica_groups=mesh['row'=32,'col'=16] {'row'}, dimensions={1}, use_global_device_ids=true | all-gather | bytes 135168 | tf_op jit(solution)/shard_map/all_gather | solution.py:46
  76.2 0.5 copy.51
  76.8 0.6 copy-done.5
  77.6 0.8 reshape.118
  78.4 7.3 all-to-all-start
  85.7 0.7 copy-done.4
  86.4 1.3 dynamic-slice
  88.3 0.2 dynamic-update-slice
  88.6 50.5 %all-reduce = bf16[2048]{0:T(1024)(128)(2,1)S(1)} all-reduce(bf16[2048]{0:T(1024)(128)(2,1)S(1)} %dynamic-update-slice), channel_id=3, replica_groups=mesh['row'=32,'col'=16] {'row'}, use_global_device_ids=true, to_apply=%add | all-reduce | flops 2048 | bytes 8192 | tf_op jit(solution)/shard_map/all_gather | solution.py:47
  139.3 0.2 dynamic-update-slice.1
  139.5 46.4 %all-reduce.1 = bf16[2048]{0:T(1024)(128)(2,1)S(1)} all-reduce(bf16[2048]{0:T(1024)(128)(2,1)S(1)} %dynamic-update-slice.1), channel_id=1, replica_groups=mesh['row'=32,'col'=16] {'row'}, use_global_device_ids=true, to_apply=%add.1 | all-reduce | flops 2048 | bytes 8192
  186.1 74.1 %psum.42 = f32[64]{0:T(128)S(1)} all-reduce(f32[64]{0:T(128)S(1)} %convolution_bitcast_fusion.9), channel_id=1, replica_groups=mesh['row'=32,'col'=16] {'col'}, use_global_device_ids=true, to_apply=%region_2.3 | all-reduce | flops 64 | bytes 512 | tf_op jit(solution)/shard_map/psum | solution.py:42
  260.2 0.2 dynamic-update-slice.2
  260.5 47.5 %all-reduce.2 = bf16[2048]{0:T(1024)(128)(2,1)S(1)} all-reduce(bf16[2048]{0:T(1024)(128)(2,1)S(1)} %dynamic-update-slice.2), channel_id=1, replica_groups=mesh['row'=32,'col'=16] {'row'}, use_global_device_ids=true, to_apply=%add.2 | all-reduce | flops 2048 | bytes 8192
  308.1 0.2 dynamic-update-slice.3
  308.3 47.3 %all-reduce.3 = bf16[2048]{0:T(1024)(128)(2,1)S(1)} all-reduce(bf16[2048]{0:T(1024)(128)(2,1)S(1)} %dynamic-update-slice.3), channel_id=1, replica_groups=mesh['row'=32,'col'=16] {'row'}, use_global_device_ids=true, to_apply=%add.3 | all-reduce | flops 2048 | bytes 8192
  355.8 0.2 reshape.119
  356.3 0.7 copy.54
  357.0 30.7 %all-to-all-start.1 = ((bf16[16,128,32]{1,2,0:T(8,128)(2,1)}), bf16[16,128,32]{1,2,0:T(8,128)(2,1)S(1)}, u32[]{:S(2)}, u32[]{:S(2)}) async-start(bf16[16,128,32]{1,2,0:T(8,128)(2,1)} %copy.54), calls=%async_computation.1 | async-start | bytes 262144 | tf_op jit(solution)/shard_map/all_to_all | solution.py:62
  388.0 33.0 %psum.43 = f32[64]{0:T(128)S(1)} all-reduce(f32[64]{0:T(128)S(1)} %convolution_bitcast_fusion.2), channel_id=1, replica_groups=mesh['row'=32,'col'=16] {'col'}, use_global_device_ids=true, to_apply=%region_3.4 | all-reduce | flops 64 | bytes 512 | tf_op jit(solution)/shard_map/psum | solution.py:42
  421.1 0.8 copy.67
  422.0 0.2 dynamic-update-slice.4
  422.3 47.8 %all-reduce.4 = bf16[2048]{0:T(1024)(128)(2,1)S(1)} all-reduce(bf16[2048]{0:T(1024)(128)(2,1)S(1)} %dynamic-update-slice.4), channel_id=1, replica_groups=mesh['row'=32,'col'=16] {'row'}, use_global_device_ids=true, to_apply=%add.4 | all-reduce | flops 2048 | bytes 8192
  470.0 38.3 %reduce-scatter.7.cloned.1.call-done = f32[32,64]{1,0:T(8,128)} async-done(((f32[512,64]{1,0:T(8,128)}), f32[32,64]{1,0:T(8,128)}) %reduce-scatter.7.cloned.1.call-update) | async-done | bytes 8208
  508.4 0.8 copy.68
  509.3 50.2 %all-gather.2 = bf16[32,64,32]{1,2,0:T(8,128)(2,1)S(1)} all-gather(bf16[1,64,32]{1,2,0:T(8,128)(2,1)S(1)} %copy.55), channel_id=1, replica_groups=mesh['row'=32,'col'=16] {'row'}, dimensions={0}, use_global_device_ids=true | all-gather | bytes 135168 | tf_op jit(solution)/shard_map/all_gather | solution.py:46
  559.5 0.3 reshape.75
  559.8 0.2 convolution_convert_fusion.1
  560.1 0.8 reshape.120
  560.9 9.8 all-to-all-start.2
  570.9 0.2 dynamic-update-slice.5
  571.1 50.5 %all-reduce.5 = bf16[2048]{0:T(1024)(128)(2,1)S(1)} all-reduce(bf16[2048]{0:T(1024)(128)(2,1)S(1)} %dynamic-update-slice.5), channel_id=1, replica_groups=mesh['row'=32,'col'=16] {'row'}, use_global_device_ids=true, to_apply=%add.5 | all-reduce | flops 2048 | bytes 8192
  621.9 0.2 reshape.121
  622.4 0.7 copy.59
  623.1 34.9 %all-to-all-start.3 = ((bf16[16,128,32]{1,2,0:T(8,128)(2,1)}), bf16[16,128,32]{1,2,0:T(8,128)(2,1)S(1)}, u32[]{:S(2)}, u32[]{:S(2)}) async-start(bf16[16,128,32]{1,2,0:T(8,128)(2,1)} %copy.59), calls=%async_computation.3 | async-start | bytes 262144 | tf_op jit(solution)/shard_map/all_to_all | solution.py:62
  658.4 0.6 pad_maximum_fusion.1
  659.1 6.6 all-to-all-done.3
  666.0 0.8 copy.69
  667.0 81.0 %reduce-scatter.9.cloned.1.call-done = f32[32,64]{1,0:T(8,128)} async-done(((f32[512,64]{1,0:T(8,128)}), f32[32,64]{1,0:T(8,128)}) %reduce-scatter.9.cloned.1.call-update) | async-done | bytes 8208
  748.0 0.8 copy.70
  748.9 50.5 %all-gather.3 = bf16[32,64,32]{1,2,0:T(8,128)(2,1)S(1)} all-gather(bf16[1,64,32]{1,2,0:T(8,128)(2,1)S(1)} %copy.62), channel_id=1, replica_groups=mesh['row'=32,'col'=16] {'row'}, dimensions={0}, use_global_device_ids=true | all-gather | bytes 135168 | tf_op jit(solution)/shard_map/all_gather | solution.py:46
  799.5 0.3 reshape.77
  799.8 0.2 convolution_convert_fusion
  800.1 0.8 reshape.122
  800.9 9.4 all-to-all-start.4
  810.5 0.2 convolution_bitcast_fusion.5
  810.8 0.2 convolution_add_fusion.1
  811.0 13.1 %all-to-all-done.4 = bf16[32,2,1024]{2,1,0:T(2,128)(2,1)S(1)} async-done(((bf16[32,2,1024]{2,1,0:T(2,128)(2,1)}), bf16[32,2,1024]{2,1,0:T(2,128)(2,1)S(1)}, u32[]{:S(2)}, u32[]{:S(2)}) %all-to-all-start.4) | async-done | bytes 131104 | tf_op jit(solution)/shard_map/all_to_all | solution.py:58
  824.1 0.2 reshape.123
  824.6 0.7 copy.65
  825.3 22.6 %all-to-all-start.5 = ((bf16[16,128,32]{1,2,0:T(8,128)(2,1)}), bf16[16,128,32]{1,2,0:T(8,128)(2,1)S(1)}, u32[]{:S(2)}, u32[]{:S(2)}) async-start(bf16[16,128,32]{1,2,0:T(8,128)(2,1)} %copy.65), calls=%async_computation.5 | async-start | bytes 262144 | tf_op jit(solution)/shard_map/all_to_all | solution.py:62
  847.9 0.2 fusion.3
  848.1 0.6 pad_maximum_fusion
  848.7 6.8 all-to-all-done.5
  855.5 0.2 fusion.2
  855.8 60.2 %all-reduce.6 = (f32[128]{0:T(128)S(1)}, f32[16,512]{1,0:T(8,128)S(1)}, f32[16]{0:T(128)S(1)}) all-reduce(f32[128]{0:T(128)S(1)} %fusion.4, f32[16,512]{1,0:T(8,128)S(1)} %convolution_add_fusion.2, f32[16]{0:T(128)S(1)} %fusion.2), channel_id=1, replica_groups=mesh['row'=32,'col'=16] {'col'}, use_global_device_ids=true, to_apply=%region_5.6 | all-reduce | flops 8336 | bytes 66688 | tf_op jit(solution)/shard_map/psum | solution.py:81
  916.1 0.6 broadcast_multiply_fusion
  916.7 0.8 fusion.1
  917.6 0.6 copy-done.6
  918.2 0.5 sub.23
  918.7 0.5 broadcast_multiply_fusion.1
  919.2 142.4 %all-reduce.9.cloned.1.call-done = bf16[128,512]{0,1:T(8,128)(2,1)} async-done(((bf16[128,512]{0,1:T(8,128)(2,1)}), bf16[128,512]{0,1:T(8,128)(2,1)}) %all-reduce.9.cloned.1.call-update) | async-done | bytes 131088 | tf_op jit(solution)/shard_map/psum | solution.py:78
  1061.7 1.3 convert_subtract_fusion.2
  (71 shorter events, 4.7 us)
Async XLA Ops:
  7.2 7.2 copy-start.2
  76.2 1.1 copy-start.5
  78.4 277.4 %all-to-all-start = ((bf16[32,2,1024]{2,1,0:T(2,128)(2,1)}), bf16[32,2,1024]{2,1,0:T(2,128)(2,1)S(1)}, u32[]{:S(2)}, u32[]{:S(2)}) async-start(bf16[32,2,1024]{2,1,0:T(2,128)(2,1)} %reshape.118), calls=%async_computation | async-start | bytes 262144 | tf_op jit(solution)/shard_map/all_to_all | solution.py:58
  85.7 0.7 copy-start.4
  139.1 46.8 %copy-start.1 = (bf16[3,64,128]{2,1,0:T(8,128)(2,1)S(1)}, bf16[3,64,128]{2,1,0:T(8,128)(2,1)}, u32[]{:S(2)}) copy-start(bf16[3,64,128]{2,1,0:T(8,128)(2,1)} %param.12) | copy-start | bytes 147460
  357.0 64.0 %all-to-all-start.1 = ((bf16[16,128,32]{1,2,0:T(8,128)(2,1)}), bf16[16,128,32]{1,2,0:T(8,128)(2,1)S(1)}, u32[]{:S(2)}, u32[]{:S(2)}) async-start(bf16[16,128,32]{1,2,0:T(8,128)(2,1)} %copy.54), calls=%async_computation.1 | async-start | bytes 262144 | tf_op jit(solution)/shard_map/all_to_all | solution.py:62
  387.7 120.7 %reduce-scatter.7.cloned.1.call-start = ((), (), s32[]{:S(2)}) async-start(), calls=%async_computation.9 | async-start | bytes 278528
  560.9 61.0 %all-to-all-start.2 = ((bf16[32,2,1024]{2,1,0:T(2,128)(2,1)}), bf16[32,2,1024]{2,1,0:T(2,128)(2,1)S(1)}, u32[]{:S(2)}, u32[]{:S(2)}) async-start(bf16[32,2,1024]{2,1,0:T(2,128)(2,1)} %reshape.120), calls=%async_computation.2 | async-start | bytes 262144 | tf_op jit(solution)/shard_map/all_to_all | solution.py:58
  570.7 50.9 %copy-start = (bf16[128,3,128]{2,0,1:T(8,128)(2,1)S(1)}, bf16[128,3,128]{2,0,1:T(8,128)(2,1)}, u32[]{:S(2)}) copy-start(bf16[128,3,128]{2,0,1:T(8,128)(2,1)} %param.13) | copy-start | bytes 294916
  623.1 42.6 %all-to-all-start.3 = ((bf16[16,128,32]{1,2,0:T(8,128)(2,1)}), bf16[16,128,32]{1,2,0:T(8,128)(2,1)S(1)}, u32[]{:S(2)}, u32[]{:S(2)}) async-start(bf16[16,128,32]{1,2,0:T(8,128)(2,1)} %copy.59), calls=%async_computation.3 | async-start | bytes 262144 | tf_op jit(solution)/shard_map/all_to_all | solution.py:62
  658.0 90.0 %reduce-scatter.9.cloned.1.call-start = ((), (), s32[]{:S(2)}) async-start(), calls=%async_computation.10 | async-start | bytes 278528
  800.9 23.2 %all-to-all-start.4 = ((bf16[32,2,1024]{2,1,0:T(2,128)(2,1)}), bf16[32,2,1024]{2,1,0:T(2,128)(2,1)S(1)}, u32[]{:S(2)}, u32[]{:S(2)}) async-start(bf16[32,2,1024]{2,1,0:T(2,128)(2,1)} %reshape.122), calls=%async_computation.4 | async-start | bytes 262144 | tf_op jit(solution)/shard_map/all_to_all | solution.py:58
  825.3 30.2 %all-to-all-start.5 = ((bf16[16,128,32]{1,2,0:T(8,128)(2,1)}), bf16[16,128,32]{1,2,0:T(8,128)(2,1)S(1)}, u32[]{:S(2)}, u32[]{:S(2)}) async-start(bf16[16,128,32]{1,2,0:T(8,128)(2,1)} %copy.65), calls=%async_computation.5 | async-start | bytes 262144 | tf_op jit(solution)/shard_map/all_to_all | solution.py:62
  847.9 213.8 %all-reduce.9.cloned.1.call-start = ((), (), s32[]{:S(2)}) async-start(), calls=%async_computation.8 | async-start | bytes 262144 | tf_op jit(solution)/shard_map/psum | solution.py:78
  917.5 144.1 %copy-start.3 = (bf16[128,32]{0,1:T(8,128)(2,1)S(1)}, bf16[128,32]{0,1:T(8,128)(2,1)}, u32[]{:S(2)}) copy-start(bf16[128,32]{0,1:T(8,128)(2,1)} %param.14) | copy-start | bytes 24580
  917.5 0.7 copy-start.6
Sparse Core Ops, SparseCore 0:
  422.1 86.2 reduce-scatter.6
  667.0 81.0 reduce-scatter.8
  917.7 143.9 all-reduce.8
